TPU v7x, 256 devices: a whole 4x4x8 slice. The times are simulated.
256 devices in a mesh: rep: 16 (over x, z_hi), grp: 16 (over y, z_lo, core).
Axes of the slice: x: 4, y: 4, z: 8 (z_hi: 4, z_lo: 2; z = z_hi * 2 + z_lo), core: 2. Of those that a mesh axis runs over, the one named last changes fastest.
Arguments:
- owners: int32 [2], replicated, may hold values from 0 to 15, as said below
- store_a: bfloat16 [16, 1024, 1024], P('rep'), may hold values from -0.1875 to 0.1875
- store_g: bfloat16 [16, 4096, 4096], P('rep', 'grp'), may hold values from -0.125 to 0.125
- vals_a: bfloat16 [16, 1024], P('rep'), may hold values from 0.29882812 to 3
- vals_g: bfloat16 [16, 4096], P('rep', 'grp'), may hold values from 0.29882812 to 3
- grads: float32 [2, 1024, 4096], P(None, 'rep', 'grp'), may hold values from -6 to 6
Outputs:
- precond: float32 [2, 1024, 4096], P(None, 'rep', 'grp')
Inputs may be any that keep to these rules, and one draw needn't show every extreme that they name: The owners of the 2 layers are distinct indices along rep; index 15 is always among them.
All inputs are finite; a program needn't handle non-finite values.
Results may differ from a plain program's by a relative error of at most 0.0003.
Values may be sent and summed in bfloat16 or wider, within the bound.
A program may use at most 64 MiB of HBM per device.

v0:
```python
import jax
import jax.numpy as jnp
from jax import lax
from jax.sharding import PartitionSpec as P

DAMPING = 0.1


def broadcast(value, axis, source):
    kept = jnp.where(lax.axis_index(axis) == source, value, 0).astype(value.dtype)
    return lax.psum(kept, axis)


def local(owners, store_a, store_g, vals_a, vals_g, grads):
    rows_r = grads.shape[1]
    width_d = store_a.shape[1]
    rep_at = lax.axis_index("rep")
    grp_at = lax.axis_index("grp")
    highest = lax.Precision.HIGHEST
    results = []
    for layer in range(grads.shape[0]):
        holder = owners[layer]
        part_rows = width_d // lax.axis_size("grp")
        own_rows = lax.dynamic_slice_in_dim(store_a[0], grp_at * part_rows, part_rows, 0)
        got_rows, got_g, got_va, got_vg = (
            broadcast(own_rows, "rep", holder),
            broadcast(store_g[0], "rep", holder),
            broadcast(vals_a[0], "rep", holder),
            broadcast(vals_g[0], "rep", holder),
        )
        basis_a = lax.all_gather(got_rows, "grp", axis=0, tiled=True).astype(jnp.float32)
        basis_g = got_g.astype(jnp.float32)
        spec_a = got_va.astype(jnp.float32)
        spec_g = got_vg.astype(jnp.float32)
        tile = grads[layer]
        turned = lax.psum_scatter(
            lax.dot_general(
                basis_g,
                tile,
                (((0,), (1,)), ((), ())),
                precision=highest,
                preferred_element_type=jnp.float32,
            ),
            "grp",
            scatter_dimension=0,
            tiled=True,
        )
        a_rows = lax.dynamic_slice_in_dim(basis_a, rep_at * rows_r, rows_r, 0)
        rotated = lax.psum_scatter(
            lax.dot_general(
                a_rows,
                turned,
                (((0,), (1,)), ((), ())),
                precision=highest,
                preferred_element_type=jnp.float32,
            ),
            "rep",
            scatter_dimension=0,
            tiled=True,
        )
        spec_rows = lax.dynamic_slice_in_dim(spec_a, rep_at * rows_r, rows_r, 0)
        scaled = rotated / (spec_rows[:, None] * spec_g[None, :] + DAMPING)
        mixed = lax.dot_general(
            lax.all_gather(scaled, "grp", axis=1, tiled=True),
            basis_g,
            (((1,), (1,)), ((), ())),
            precision=highest,
            preferred_element_type=jnp.float32,
        )
        block = lax.dynamic_slice(
            basis_a, (0, rep_at * rows_r), (lax.axis_size("rep") * rows_r, rows_r)
        )
        results.append(
            lax.psum_scatter(
                jnp.dot(block, mixed, precision=highest, preferred_element_type=jnp.float32),
                "rep",
                scatter_dimension=0,
                tiled=True,
            )
        )
    return jnp.stack(results)


def solution(mesh):
    return jax.shard_map(
        local,
        mesh=mesh,
        in_specs=(
            P(),
            P("rep", None, None),
            P("rep", "grp", None),
            P("rep", None),
            P("rep", "grp"),
            P(None, "rep", "grp"),
        ),
        out_specs=P(None, "rep", "grp"),
        check_vma=False,
    )
```

profile of v0, /device:TPU:1, one launch (start us, length us, event | category | flops | bytes accessed | tf_op | source)
XLA Modules:
  0.0 895.2 jit_solution(8994822031895040651)
XLA Ops:
  6.5 0.0 all-reduce.4.cloned.1.call-start
  6.5 1.4 fusion.22
  9.2 3.8 select_bitcast_fusion.1
  13.0 1.7 select_bitcast_fusion.3
  14.7 0.0 copy-start.1
  14.7 0.0 all-reduce.4.cloned.1.call-update
  14.7 0.0 reduce-scatter.7.cloned.1.call-start
  14.8 231.9 %all-reduce.4.cloned.1.call-done = (bf16[256,4096]{1,0:T(8,128)(2,1)}, bf16[64,1024]{1,0:T(8,128)(2,1)}, bf16[256,4096]{1,0:T(8,128)(2,1)}, bf16[64,1024]{1,0:T(8,128)(2,1)}) async-done(((bf16[256,4096]{1,0:T(8,128)(2,1)}, bf16[64,1024]{1,0:T(8,128)(2,1)}, bf16[256,4096]{1,0:T(8,128)(2,1)}, bf16[64,1024]{1,0:T(8,128)(2,1)}), (bf16[256,4096]{1,0:T(8,128)(2,1)}, bf16[64,1024]{1,0:T(8,128)(2,1)}, ...) | async-done | bytes 4456464 | tf_op jit(solution)/shard_map/psum | solution.py:11
  246.7 0.0 copy-done.1
  246.7 5.3 fusion.10
  251.9 0.0 copy-start
  251.9 0.0 reduce-scatter.7.cloned.1.call-update
  251.9 0.0 all-gather.5.cloned.1.call-start
  252.0 0.7 all-gather.5.cloned.1.call-update
  252.7 0.0 reduce-scatter.13.cloned.1.call-start
  252.7 0.8 copy-done
  253.5 3.6 fusion.8
  257.2 0.0 reduce-scatter.13.cloned.1.call-update
  257.2 0.0 all-gather.9.cloned.1.call-start
  257.2 0.5 all-gather.9.cloned.1.call-update
  257.8 0.0 reduce-scatter.9.cloned.1.call-start
  257.8 0.0 copy-start.3
  257.8 0.0 copy-start.2
  257.9 58.2 %reduce-scatter.7.cloned.1.call-done = f32[256,64]{1,0:T(8,128)} async-done(((f32[4096,64]{1,0:T(8,128)}), f32[256,64]{1,0:T(8,128)}) %reduce-scatter.7.cloned.1.call-update) | async-done | bytes 65552 | tf_op jit(solution)/shard_map/reduce_scatter | solution.py:36
  316.1 40.1 %all-gather.5.cloned.1.call-done = bf16[1024,1024]{1,0:T(8,128)(2,1)} async-done(((bf16[64,1024]{1,0:T(8,128)(2,1)}), bf16[1024,1024]{1,0:T(8,128)(2,1)}) %all-gather.5.cloned.1.call-update) | async-done | bytes 2097168 | tf_op jit(solution)/shard_map/all_gather | solution.py:31
  356.1 2.6 fusion.6
  358.8 0.0 reduce-scatter.9.cloned.1.call-update
  358.8 0.0 reduce-scatter.15.cloned.1.call-start
  358.9 63.3 %reduce-scatter.13.cloned.1.call-done = f32[256,64]{1,0:T(8,128)} async-done(((f32[4096,64]{1,0:T(8,128)}), f32[256,64]{1,0:T(8,128)}) %reduce-scatter.13.cloned.1.call-update) | async-done | bytes 65552 | tf_op jit(solution)/shard_map/reduce_scatter | solution.py:36
  422.2 40.0 %all-gather.9.cloned.1.call-done = bf16[1024,1024]{1,0:T(8,128)(2,1)} async-done(((bf16[64,1024]{1,0:T(8,128)(2,1)}), bf16[1024,1024]{1,0:T(8,128)(2,1)}) %all-gather.9.cloned.1.call-update) | async-done | bytes 2097168 | tf_op jit(solution)/shard_map/all_gather | solution.py:31
  462.2 2.6 fusion.4
  464.8 0.0 reduce-scatter.15.cloned.1.call-update
  464.8 0.0 all-gather.7.cloned.1.call-start
  464.8 0.0 copy-done.3
  464.9 0.0 copy-done.2
  464.9 38.2 %all-reduce = (bf16[1024]{0:T(1024)(128)(2,1)S(1)}, bf16[1024]{0:T(1024)(128)(2,1)S(1)}, bf16[256]{0:T(256)(128)(2,1)S(1)}, bf16[256]{0:T(256)(128)(2,1)S(1)}) all-reduce(bf16[1024]{0:T(1024)(128)(2,1)S(1)} %get-tuple-element.5, bf16[1024]{0:T(1024)(128)(2,1)S(1)} %get-tuple-element.6, ...), channel_id=1, replica_groups=mesh['rep'=16,'grp'=16] {'rep'}, use_global_device_ids=true, to_apply=%region_4.5 | all-reduce | flops 2560 | bytes 10240 | tf_op jit(solution)/shard_map/psum | solution.py:11
  503.2 0.1 dynamic_slice.25
  503.2 47.0 %reduce-scatter.9.cloned.1.call-done = f32[64,256]{1,0:T(8,128)} async-done(((f32[1024,256]{1,0:T(8,128)}), f32[64,256]{1,0:T(8,128)}) %reduce-scatter.9.cloned.1.call-update) | async-done | bytes 65552 | tf_op jit(solution)/shard_map/reduce_scatter | solution.py:49
  550.2 1.5 add_divide_fusion.1
  551.8 0.0 all-gather.7.cloned.1.call-update
  551.8 0.0 all-gather.11.cloned.1.call-start
  551.9 0.1 dynamic_slice.28
  551.9 86.0 %reduce-scatter.15.cloned.1.call-done = f32[64,256]{1,0:T(8,128)} async-done(((f32[1024,256]{1,0:T(8,128)}), f32[64,256]{1,0:T(8,128)}) %reduce-scatter.15.cloned.1.call-update) | async-done | bytes 65552 | tf_op jit(solution)/shard_map/reduce_scatter | solution.py:49
  637.9 1.6 add_divide_fusion
  639.4 0.0 all-gather.11.cloned.1.call-update
  639.5 0.0 reduce-scatter.11.cloned.1.call-start
  639.5 35.3 %all-gather.7.cloned.1.call-done = f32[64,4096]{1,0:T(8,128)} async-done(((f32[64,256]{1,0:T(8,128)}), f32[64,4096]{1,0:T(8,128)}) %all-gather.7.cloned.1.call-update) | async-done | bytes 1048592 | tf_op jit(solution)/shard_map/all_gather | solution.py:64
  674.8 3.9 fusion.23
  678.8 2.5 fusion.2
  681.3 0.0 reduce-scatter.11.cloned.1.call-update
  681.3 0.0 reduce-scatter.17.cloned.1.call-start
  681.4 30.5 %all-gather.11.cloned.1.call-done = f32[64,4096]{1,0:T(8,128)} async-done(((f32[64,256]{1,0:T(8,128)}), f32[64,4096]{1,0:T(8,128)}) %all-gather.11.cloned.1.call-update) | async-done | bytes 1048592 | tf_op jit(solution)/shard_map/all_gather | solution.py:64
  711.9 3.2 fusion.24
  715.1 2.6 fusion
  717.7 0.0 reduce-scatter.17.cloned.1.call-update
  717.7 81.9 %reduce-scatter.11.cloned.1.call-done = f32[64,256]{1,0:T(8,128)} async-done(((f32[1024,256]{1,0:T(8,128)}), f32[64,256]{1,0:T(8,128)}) %reduce-scatter.11.cloned.1.call-update) | async-done | bytes 65552 | tf_op jit(solution)/shard_map/reduce_scatter | solution.py:74
  799.6 87.5 %reduce-scatter.17.cloned.1.call-done = f32[64,256]{1,0:T(8,128)} async-done(((f32[1024,256]{1,0:T(8,128)}), f32[64,256]{1,0:T(8,128)}) %reduce-scatter.17.cloned.1.call-update) | async-done | bytes 65552 | tf_op jit(solution)/shard_map/reduce_scatter | solution.py:74
  887.1 1.5 pad_maximum_fusion
  (4 shorter events, 0.1 us)
Async XLA Ops:
  6.5 240.1 %all-reduce.4.cloned.1.call-start = ((), (), s32[]{:S(2)}) async-start(), calls=%async_computation.16 | async-start | bytes 8912896 | tf_op jit(solution)/shard_map/psum | solution.py:11
  14.7 232.0 %copy-start.1 = (f32[2,64,256]{2,1,0:T(8,128)S(1)}, f32[2,64,256]{2,1,0:T(8,128)}, u32[]{:S(2)}) copy-start(f32[2,64,256]{2,1,0:T(8,128)} %param.11) | copy-start | bytes 393220
  14.7 301.4 %reduce-scatter.7.cloned.1.call-start = ((), (), s32[]{:S(2)}) async-start(), calls=%async_computation.7 | async-start | bytes 2228224 | tf_op jit(solution)/shard_map/reduce_scatter | solution.py:36
  251.9 1.6 copy-start
  251.9 104.2 %all-gather.5.cloned.1.call-start = ((), (), s32[]{:S(2)}) async-start(), calls=%async_computation.6 | async-start | bytes 2228224 | tf_op jit(solution)/shard_map/all_gather | solution.py:31
  252.7 169.5 %reduce-scatter.13.cloned.1.call-start = ((), (), s32[]{:S(2)}) async-start(), calls=%async_computation.12 | async-start | bytes 2228224 | tf_op jit(solution)/shard_map/reduce_scatter | solution.py:36
  257.2 205.0 %all-gather.9.cloned.1.call-start = ((), (), s32[]{:S(2)}) async-start(), calls=%async_computation.11 | async-start | bytes 2228224 | tf_op jit(solution)/shard_map/all_gather | solution.py:31
  257.8 292.5 %reduce-scatter.9.cloned.1.call-start = ((), (), s32[]{:S(2)}) async-start(), calls=%async_computation.8 | async-start | bytes 1114112 | tf_op jit(solution)/shard_map/reduce_scatter | solution.py:49
  257.8 207.0 %copy-start.3 = (bf16[1,256]{1,0:T(2,128)(2,1)S(1)}, bf16[1,256]{1,0:T(2,128)(2,1)}, u32[]{:S(2)}) copy-start(bf16[1,256]{1,0:T(2,128)(2,1)} %param.10) | copy-start | bytes 1540
  257.8 207.0 %copy-start.2 = (bf16[1,1024]{1,0:T(2,128)(2,1)S(1)}, bf16[1,1024]{1,0:T(2,128)(2,1)}, u32[]{:S(2)}) copy-start(bf16[1,1024]{1,0:T(2,128)(2,1)} %param.9) | copy-start | bytes 6148
  358.8 279.1 %reduce-scatter.15.cloned.1.call-start = ((), (), s32[]{:S(2)}) async-start(), calls=%async_computation.13 | async-start | bytes 1114112 | tf_op jit(solution)/shard_map/reduce_scatter | solution.py:49
  464.8 210.1 %all-gather.7.cloned.1.call-start = ((), (), s32[]{:S(2)}) async-start(), calls=%async_computation.9 | async-start | bytes 1114112 | tf_op jit(solution)/shard_map/all_gather | solution.py:64
  551.8 160.0 %all-gather.11.cloned.1.call-start = ((), (), s32[]{:S(2)}) async-start(), calls=%async_computation.14 | async-start | bytes 1114112 | tf_op jit(solution)/shard_map/all_gather | solution.py:64
  639.5 160.1 %reduce-scatter.11.cloned.1.call-start = ((), (), s32[]{:S(2)}) async-start(), calls=%async_computation.10 | async-start | bytes 1114112 | tf_op jit(solution)/shard_map/reduce_scatter | solution.py:74
  681.3 205.8 %reduce-scatter.17.cloned.1.call-start = ((), (), s32[]{:S(2)}) async-start(), calls=%async_computation.15 | async-start | bytes 1114112 | tf_op jit(solution)/shard_map/reduce_scatter | solution.py:74
Sparse Core Ops, SparseCore 0:
  14.8 231.7 all-reduce.3
  252.1 63.9 reduce-scatter.6
  318.1 38.0 all-gather.4
  358.7 63.4 reduce-scatter.12
  424.0 38.0 all-gather.8
  465.9 84.2 reduce-scatter.8
  553.7 84.1 reduce-scatter.14
  639.8 34.9 all-gather.6
  676.8 35.0 all-gather.10
  715.6 83.9 reduce-scatter.10
  803.1 83.9 reduce-scatter.16
where the time goes:
time: 897 us; the launch traced here: 895 us
  waiting for transfers between devices  803 us (90%)
  blocking collectives  38.2 us (4%)
  matrix products  26.4 us (3%)
  between operations  14.6 us (2%)
  other arithmetic  10.2 us (1%)
    psum x1, waiting for transfers between devices, broadcast(): return lax.psum(kept, axis)  232 us
    reduce_scatter x2, waiting for transfers between devices, local(): lax.psum_scatter(jnp.dot(block, mixed, precision=highest, preferred_eleme...  169 us
    reduce_scatter x2, waiting for transfers between devices, local(): lax.psum_scatter(lax.dot_general(a_rows, turned, (((0,), (1,)), ((), ()))...  133 us
    reduce_scatter x2, waiting for transfers between devices, local(): lax.psum_scatter(lax.dot_general(basis_g, tile, (((0,), (1,)), ((), ())),...  122 us
    all_gather x2, waiting for transfers between devices, local(): lax.all_gather(got_rows, 'grp', axis=0, tiled=True).astype(jnp.float32)  80.1 us
    all_gather x2, waiting for transfers between devices, local(): lax.all_gather(scaled, 'grp', axis=1, tiled=True)  65.8 us
    psum x1, blocking collectives, broadcast(): return lax.psum(kept, axis)  38.2 us
  transfers between devices with their start and end apart: 11, of which 11 were waited for; matrix products, arithmetic and copies ran while one was open for 3% of the time, Pallas kernels for 0%

commit v1 on v0

v1 whole, which is shorter than its diff:
```python
import functools

import jax
import jax.numpy as jnp
from jax import lax
from jax.experimental import pallas as pl
from jax.experimental.pallas import tpu as pltpu
from jax.sharding import PartitionSpec as P

DAMPING = 0.1
MESH = pl.DeviceIdType.MESH
NX, NZ, NY, NL, NC = 4, 4, 4, 2, 2
FIXED_OWNER = 15
CHUNKS = 4
BF16, F32 = jnp.bfloat16, jnp.float32


def coords():
    rep, grp = lax.axis_index("rep"), lax.axis_index("grp")
    return rep // NZ, rep % NZ, grp // (NL * NC), (grp // NC) % NL, grp % NC


def dev(x, zh, y, zl, c):
    return (x * NZ + zh, y * (NL * NC) + zl * NC + c)


def greet(peers):
    barrier = pltpu.get_barrier_semaphore()
    for peer in peers:
        pl.semaphore_signal(barrier, inc=1, device_id=peer, device_id_type=MESH)
    pl.semaphore_wait(barrier, len(peers))


def spread_kernel(other, sg, qap, gt, qg, qa, gx, qg_ss, qg_rs, fw_ss, qa_ss, qa_rs, qf_ss, ql_ss, ql_rs, qy_ss, qy_rs,
                  gx_ss, gx_rs, gc_ss, gc_rs, loc):
    x, zh, y, zl, c = coords()
    x_peers = [(x + d) % NX for d in range(1, NX)]
    peers = [dev(p, zh, y, zl, k) for p in x_peers for k in range(NC)]
    peers += [dev(x, zh, y, zl, 1 - c), dev(x, (zh + 1) % NZ, y, zl, c), dev(x, (zh + 3) % NZ, y, zl, c)]
    peers += [dev(x, zh, y, 1 - zl, c)] + [dev(x, zh, (y + d) % NY, zl, c) for d in range(1, NY)]
    greet(peers)

    rows = 256 // CHUNKS
    owners = (FIXED_OWNER, other)
    slot = y * (NL * NC) + zl * NC + c

    def mine(layer):
        return (x == owners[layer] // NZ) & (zh == owners[layer] % NZ)

    def remote(src, dst, ss, rs, to):
        return pltpu.make_async_remote_copy(src_ref=src, dst_ref=dst, send_sem=ss, recv_sem=rs, device_id=to,
                                            device_id_type=MESH)

    def qa_first(layer, d):
        ox, oz = owners[layer] // NZ, owners[layer] % NZ
        return remote(qap, qa.at[slot], qa_ss.at[layer, d], qa_rs.at[c], dev((ox + d) % NX, oz, y, zl, layer))

    def qa_local():
        return pltpu.make_async_copy(qap, qa.at[slot], qa_rs.at[c])

    def qg_first(layer, k, d, core):
        ox, oz = owners[layer] // NZ, owners[layer] % NZ
        tx = (ox + d) % NX
        return remote(sg.at[pl.ds(k * rows, rows), pl.ds((tx * NC + core) * 512, 512)],
                      qg.at[layer, pl.ds(pl.multiple_of(c * 256 + k * rows, rows), rows), :],
                      qg_ss.at[layer, k, d, core], qg_rs.at[layer, c, k], dev(tx, oz, y, zl, core))

    def qg_local(layer, k, core):
        ox = owners[layer] // NZ
        return pltpu.make_async_copy(sg.at[pl.ds(k * rows, rows), pl.ds((ox * NC + core) * 512, 512)],
                                     qg.at[layer, pl.ds(core * 256 + k * rows, rows), :], qg_rs.at[layer, core, k])

    order = (2, 1, 3, 0)
    for layer in range(2):
        @pl.when(mine(layer))
        def _():
            for d in order:
                if d:
                    qa_first(layer, d).start()
                else:
                    @pl.when(c == layer)
                    def _():
                        qa_local().start()

                    @pl.when(c != layer)
                    def _():
                        qa_first(layer, 0).start()

    g_own = [pltpu.make_async_copy(gt.at[l], gx.at[l, pl.ds(pl.multiple_of(x * 64, 64), 64),
                                                   pl.ds(pl.multiple_of(c * 256, 256), 256)], loc.at[l]) for l in range(2)]
    g_x = [[remote(gt.at[l], gx.at[l, pl.ds(pl.multiple_of(x * 64, 64), 64), pl.ds(pl.multiple_of(c * 256, 256), 256)],
                   gx_ss.at[l, d - 1], gx_rs.at[l, d - 1], dev((x + d) % NX, zh, y, zl, c)) for d in range(1, NX)]
           for l in range(2)]
    for l in range(2):
        g_own[l].start()
        for copy in g_x[l]:
            copy.start()

    for k in range(CHUNKS):
        for layer in range(2):
            @pl.when(mine(layer))
            def _():
                for d in order:
                    for core in range(NC):
                        if d:
                            qg_first(layer, k, d, core).start()
                        else:
                            @pl.when(c == core)
                            def _():
                                qg_local(layer, k, core).start()

                            @pl.when(c != core)
                            def _():
                                qg_first(layer, k, 0, core).start()

    def forward(part, layer):
        oz = owners[layer] % NZ
        if part == 0:
            return (zh + 1) % NZ, (zh + NZ - oz) % NZ < NZ - 1
        return (zh + NZ - 1) % NZ, (oz + NZ - zh) % NZ < NZ - 1

    def qa_on(layer, part):
        nxt, _ = forward(part, layer)
        s = y * (NL * NC) + zl * NC + part
        return remote(qa.at[s], qa.at[s], qf_ss.at[part], qa_rs.at[part], dev(x, nxt, y, zl, layer))

    for layer in range(2):
        @pl.when(c == layer)
        def _():
            for part in range(2):
                copy = qa_on(layer, part)
                copy.wait_recv()

                @pl.when(forward(part, layer)[1])
                def _():
                    copy.start()

    two = pl.ds(y * (NL * NC) + zl * NC, NC)
    two_in = pl.ds(y * (NL * NC) + (1 - zl) * NC, NC)
    four = pl.ds(y * (NL * NC), NL * NC)
    qa_l = remote(qa.at[two], qa.at[two], ql_ss, ql_rs, dev(x, zh, y, 1 - zl, c))
    qa_l.start()

    def qg_on(layer, part, k):
        nxt, _ = forward(part, layer)
        block = qg.at[layer, pl.ds(part * 256 + k * rows, rows), :]
        return remote(block, block, fw_ss.at[layer, part, k], qg_rs.at[layer, part, k], dev(x, nxt, y, zl, c))

    def pass_chunk(k):
        for layer in range(2):
            for part in range(2):
                copy = qg_on(layer, part, k)
                copy.wait_recv()

                @pl.when(forward(part, layer)[1])
                def _():
                    copy.start()

    pass_chunk(0)
    g_c = []
    for l in range(2):
        g_own[l].wait()
        for copy in g_x[l]:
            copy.wait_recv()
        half = gx.at[l, :, pl.ds(pl.multiple_of(c * 256, 256), 256)]
        g_c.append(remote(half, half, gc_ss.at[l], gc_rs.at[l], dev(x, zh, y, zl, 1 - c)))
        g_c[l].start()
    qa_l.wait_recv()
    qa_y = [remote(qa.at[four], qa.at[four], qy_ss.at[d - 1], qy_rs.at[d - 1], dev(x, zh, (y + d) % NY, zl, c))
            for d in range(1, NY)]
    for copy in qa_y:
        copy.start()
    for k in range(1, CHUNKS):
        pass_chunk(k)

    for l in range(2):
        g_c[l].wait()
        for copy in g_x[l]:
            copy.wait_send()
    for copy in qa_y:
        copy.wait()
    qa_l.wait_send()
    for layer in range(2):
        for part in range(2):
            @pl.when(forward(part, layer)[1])
            def _():
                @pl.when(c == layer)
                def _():
                    qa_on(layer, part).wait_send()
                for k in range(CHUNKS):
                    qg_on(layer, part, k).wait_send()

        @pl.when(mine(layer))
        def _():
            for d in order:
                if d:
                    qa_first(layer, d).wait_send()
                else:
                    @pl.when(c != layer)
                    def _():
                        qa_first(layer, 0).wait_send()
            for k in range(CHUNKS):
                for d in order:
                    for core in range(NC):
                        if d:
                            qg_first(layer, k, d, core).wait_send()
                        else:
                            @pl.when(c != core)
                            def _():
                                qg_first(layer, k, 0, core).wait_send()


def spread(other, sg, qap, gt):
    dma = pltpu.SemaphoreType.DMA
    anywhere = pl.BlockSpec(memory_space=pl.ANY)
    return pl.pallas_call(
        functools.partial(spread_kernel, other),
        out_shape=(
            jax.ShapeDtypeStruct((2, 512, 512), BF16),
            jax.ShapeDtypeStruct((16, 80, 1024), BF16),
            jax.ShapeDtypeStruct((2, 256, 512), F32),
        ),
        in_specs=[anywhere] * 3,
        out_specs=(anywhere,) * 3,
        scratch_shapes=[
            dma((2, CHUNKS, NX, NC)), dma((2, NC, CHUNKS)), dma((2, 2, CHUNKS)),
            dma((2, NX)), dma((2,)), dma((2,)),
            dma, dma, dma((3,)), dma((3,)),
            dma((2, 3)), dma((2, 3)), dma((2,)), dma((2,)), dma((2,)),
        ],
        compiler_params=pltpu.CompilerParams(collective_id=other, has_side_effects=True),
        name=f"spread_{other}",
    )(sg, qap, gt)


def split(value):
    high = value.astype(BF16)
    low = (value - high.astype(F32)).astype(BF16)
    return jnp.concatenate([high, low], axis=0)


def fold(value):
    half = value.shape[0] // 2
    return value[:half] + value[half:]


def dot(left, right, dims=((1,), (0,))):
    return lax.dot_general(left, right, (dims, ((), ())), preferred_element_type=F32)


def turn_kernel(qg, qa, gx, out, yt, yr, t4, mid, wt, wr, wall, mx, mc, ms, orc, y_ss, y_rs, t_ss, t_rs, w_ss, w_rs, a_ss,
                a_rs, c_ss, c_rs, o_ss, o_rs):
    x, zh, y, zl, c = coords()
    q = y * NL + zl

    def remote(src, dst, ss, rs, to):
        return pltpu.make_async_remote_copy(src_ref=src, dst_ref=dst, send_sem=ss, recv_sem=rs, device_id=to,
                                            device_id_type=MESH)

    near = [((y + dy) % NY, (zl + dl) % NL) for dy in range(NY) for dl in range(NL)]
    peers = [dev(x, zh, ty, tl, k) for ty, tl in near[1:] for k in range(NC)] + [dev(x, zh, y, zl, 1 - c)]
    peers += [dev((x + d) % NX, zh, y, zl, c) for d in range(1, NX)]
    peers += [dev(x, (zh + d) % NZ, y, zl, c) for d in range(1, NZ)]
    greet(peers)

    def y_copy(l, i):
        ty, tl = near[i]
        tq = ty * NL + tl
        return remote(yt.at[l, pl.ds(pl.multiple_of(tq * 64, 64), 64), :], yr.at[q, c], y_ss.at[l, i], y_rs.at[i, c],
                      dev(x, zh, ty, tl, l))

    def y_self(l):
        return pltpu.make_async_copy(yt.at[l, pl.ds(pl.multiple_of(q * 64, 64), 64), :], yr.at[q, l], y_rs.at[0, l])

    for l in range(2):
        part = fold(dot(split(gx[l]), qg[l]))
        yt[l] = part.T
        for i in range(1, 8):
            y_copy(l, i).start()

        @pl.when(c == l)
        def _():
            y_self(l).start()

        @pl.when(c != l)
        def _():
            y_copy(l, 0).start()

    def y_arrived(i, k):
        dy, dl = i // NL, i % NL
        sq = ((y + NY - dy) % NY) * NL + (zl + dl) % NL
        return remote(yr.at[sq, k], yr.at[sq, k], y_ss.at[0, i], y_rs.at[i, k], dev(x, zh, y, zl, 1 - c))

    for i in range(8):
        for k in range(NC):
            y_arrived(i, k).wait_recv()
    t4[...] = jnp.sum(yr[...], axis=0).reshape(128, 256)

    def t_copy(d):
        to = (zh + d) % NZ
        return remote(t4.at[pl.ds(pl.multiple_of(to * 32, 32), 32), :], mid.at[zh], t_ss.at[d], t_rs.at[d],
                      dev(x, to, y, zl, c))

    for d in range(1, NZ):
        t_copy(d).start()
    mid[zh] = t4[pl.ds(pl.multiple_of(zh * 32, 32), 32), :]

    spec_a = qa[0, 64:65, :].astype(F32)
    spot = (x * 2 + zh // 2) * 2 + q // 4
    line = qa[spot, 64:80, :][1:2, :256].astype(F32)
    start = (q % 4) * 64 + (zh % 2) * 32
    pick = lax.broadcasted_iota(jnp.int32, (32, 256), 1) == lax.broadcasted_iota(jnp.int32, (32, 256), 0) + start
    spec_g = jnp.sum(jnp.where(pick, line, 0.0), axis=1, keepdims=True)
    basis = qa[:, 0:64, :].reshape(1024, 1024)

    for d in range(1, NZ):
        t_copy(d).wait_recv()
    turned = jnp.concatenate([mid[k] for k in range(NZ)], axis=1)
    rotated = fold(dot(split(turned), basis))
    scaled = rotated / (spec_g * spec_a + DAMPING)
    wide = fold(dot(split(scaled), basis, ((1,), (1,))))
    for k in range(NZ):
        wt[k] = wide[:, k * 256:(k + 1) * 256]

    def w_copy(d):
        to = (zh + d) % NZ
        return remote(wt.at[to], wr.at[pl.ds(pl.multiple_of(zh * 32, 32), 32), :], w_ss.at[d], w_rs.at[d],
                      dev(x, to, y, zl, c))

    for d in range(1, NZ):
        w_copy(d).start()
    wr[pl.ds(pl.multiple_of(zh * 32, 32), 32), :] = wt[zh]
    for d in range(1, NZ):
        w_copy(d).wait_recv()

    def a_copy(k, i):
        ty, tl = near[i]
        return remote(wr.at[pl.ds(k * 64, 64), :], wall.at[c, pl.ds(pl.multiple_of(q * 64, 64), 64), :], a_ss.at[k, i],
                      a_rs.at[c, i], dev(x, zh, ty, tl, k))

    def a_self(k):
        return pltpu.make_async_copy(wr.at[pl.ds(k * 64, 64), :], wall.at[k, pl.ds(pl.multiple_of(q * 64, 64), 64), :],
                                     a_rs.at[k, 0])

    for i in range(1, 8):
        for k in range(NC):
            a_copy(k, i).start()
    for k in range(NC):
        @pl.when(c == k)
        def _():
            a_self(k).start()

        @pl.when(c != k)
        def _():
            a_copy(k, 0).start()

    def a_arrived(l, i):
        dy, dl = i // NL, i % NL
        sq = ((y + NY - dy) % NY) * NL + (zl + dl) % NL
        block = wall.at[l, pl.ds(pl.multiple_of(sq * 64, 64), 64), :]
        return remote(block, block, a_ss.at[0, i], a_rs.at[l, i], dev(x, zh, y, zl, 1 - c))

    def c_copy(l):
        return remote(mx.at[l, 1 - c], mc.at[l], c_ss.at[l], c_rs.at[l], dev(x, zh, y, zl, 1 - c))

    def o_copy(l, d):
        to = (x + d) % NX
        return remote(ms.at[l, pl.ds(pl.multiple_of(to * 64, 64), 64), :], orc.at[l, x], o_ss.at[l, d], o_rs.at[l, d],
                      dev(to, zh, y, zl, c))

    for l in range(2):
        for i in range(8):
            a_arrived(l, i).wait_recv()
        part = fold(dot(split(wall[l].T), qg[l], ((1,), (1,))))
        mx[l, 0] = part[:, :256]
        mx[l, 1] = part[:, 256:]
        c_copy(l).start()
    for l in range(2):
        c_copy(l).wait_recv()
        ms[l] = mx[l, c] + mc[l]
        for d in range(1, NX):
            o_copy(l, d).start()
        orc[l, x] = ms[l, pl.ds(pl.multiple_of(x * 64, 64), 64), :]
    for l in range(2):
        for d in range(1, NX):
            o_copy(l, d).wait_recv()
        out[l] = (orc[l, 0] + orc[l, 1]) + (orc[l, 2] + orc[l, 3])

    for l in range(2):
        for i in range(1, 8):
            y_copy(l, i).wait_send()

        @pl.when(c != l)
        def _():
            y_copy(l, 0).wait_send()
            a_copy(l, 0).wait_send()
        c_copy(l).wait_send()
        for d in range(1, NX):
            o_copy(l, d).wait_send()
        for i in range(1, 8):
            a_copy(l, i).wait_send()
    for d in range(1, NZ):
        t_copy(d).wait_send()
        w_copy(d).wait_send()


def turn(qg, qa, gx):
    dma = pltpu.SemaphoreType.DMA
    vmem = pl.BlockSpec(memory_space=pltpu.VMEM)
    return pl.pallas_call(
        turn_kernel,
        out_shape=jax.ShapeDtypeStruct((2, 64, 256), F32),
        in_specs=[vmem] * 3,
        out_specs=vmem,
        scratch_shapes=[
            pltpu.VMEM((2, 512, 256), F32),
            pltpu.VMEM((8, 2, 64, 256), F32),
            pltpu.VMEM((128, 256), F32),
            pltpu.VMEM((4, 32, 256), F32),
            pltpu.VMEM((4, 32, 256), F32),
            pltpu.VMEM((128, 256), F32),
            pltpu.VMEM((2, 512, 256), F32),
            pltpu.VMEM((2, 2, 256, 256), F32),
            pltpu.VMEM((2, 256, 256), F32),
            pltpu.VMEM((2, 256, 256), F32),
            pltpu.VMEM((2, 4, 64, 256), F32),
            dma((2, 8)), dma((8, 2)), dma((4,)), dma((4,)), dma((4,)), dma((4,)), dma((2, 8)), dma((2, 8)),
            dma((2,)), dma((2,)), dma((2, 4)), dma((2, 4)),
        ],
        compiler_params=pltpu.CompilerParams(collective_id=15, has_side_effects=True, vmem_limit_bytes=40 * 2**20),
        name="turn",
    )(qg, qa, gx)


def local(owners, store_a, store_g, vals_a, vals_g, grads):
    grp = lax.axis_index("grp")
    first = owners[0] == FIXED_OWNER
    other = jnp.where(first, owners[1], owners[0])
    tiles = jnp.where(first, grads, grads[::-1])
    block = (grp % 4) * 4 + grp // 4
    piece = jnp.concatenate(
        [
            lax.dynamic_slice_in_dim(store_a[0], block * 64, 64, 0),
            vals_a,
            jnp.pad(vals_g, ((0, 0), (0, 1024 - 256))),
            jnp.zeros((14, 1024), BF16),
        ],
        axis=0,
    )
    qg, qa, gx = lax.switch(
        other, [functools.partial(spread, k) for k in range(FIXED_OWNER)], store_g[0], piece, tiles
    )
    result = turn(qg, qa, gx)
    return jnp.where(first, result, result[::-1])


def solution(mesh):
    return jax.shard_map(
        local,
        mesh=mesh,
        in_specs=(
            P(),
            P("rep", None, None),
            P("rep", "grp", None),
            P("rep", None),
            P("rep", "grp"),
            P(None, "rep", "grp"),
        ),
        out_specs=P(None, "rep", "grp"),
        check_vma=False,
    )
```

time: 897 us -> 256 us (0.29)
  waiting for transfers between devices: 803 us -> 0 us
  Pallas kernels: 0 us -> 244 us
  blocking collectives: 38.2 us -> 0 us
  matrix products: 26.4 us -> 0 us
  between operations: 14.6 us -> 2.07 us
    reduce_scatter x6 -> x0, waiting for transfers between devices: 424 us -> none  [the longest x2 169 us: local(): lax.psum_scatter(jnp.dot(block, mixed, precision=highest, preferred_eleme...]
    pallas_call x0 -> x2, Pallas kernels: none -> 244 us  [the longest x1 158 us: spread(): pl.pallas_call(functools.partial(spread_kernel, other), out_shape=(jax.Sh...]
    psum x1 -> x0, waiting for transfers between devices: 232 us -> none  [broadcast(): return lax.psum(kept, axis)]
    all_gather x4 -> x0, waiting for transfers between devices: 146 us -> none  [the longest x2 80.1 us: local(): lax.all_gather(got_rows, 'grp', axis=0, tiled=True).astype(jnp.float32)]
    psum x1 -> x0, blocking collectives: 38.2 us -> none  [broadcast(): return lax.psum(kept, axis)]
    dot_general x8 -> x0, matrix products: 26.4 us -> none  [the longest x2 8.9 us: local(): lax.dot_general(basis_g, tile, (((0,), (1,)), ((), ())), precision=highes...]
  transfers between devices with their start and end apart: 11 -> 0, of which waited for: 11 -> 0; matrix products, arithmetic and copies ran while one was open for 3% -> 0% of each run, Pallas kernels for 0% -> 0%
where the time goes in v1:
time: 256 us; the launch traced here: 255 us
  Pallas kernels  244 us (95%)
  loops' own time  5.12 us (2%)
    pallas_call x1, Pallas kernels, spread(): pl.pallas_call(functools.partial(spread_kernel, other), out_shape=(jax.Sh...  158 us
    pallas_call x1, Pallas kernels, turn(): pl.pallas_call(turn_kernel, out_shape=jax.ShapeDtypeStruct((2, 64, 256),...  85.7 us
    another operation x1, loops' own time, local(): lax.switch(other, [functools.partial(spread, k) for k in range(FIXED_OWNE...  5.12 us

profile of v1, /device:TPU:1, one launch (start us, length us, event | category | flops | bytes accessed | tf_op | source)
XLA Modules:
  0.0 254.8 jit_solution(321620513314612004)
XLA Ops:
  0.0 0.0 copy-start
  0.0 0.1 pad.8.clone
  0.1 1.4 fusion.4
  3.5 0.0 copy-done
  3.5 0.8 fusion.3
  4.3 1.0 reverse_select_fusion.1
  5.3 163.0 %conditional.1 = ((bf16[2,512,512]{2,1,0:T(8,128)(2,1)S(1)}, bf16[16,80,1024]{2,1,0:T(8,128)(2,1)}, f32[2,256,512]{2,1,0:T(8,128)})) conditional(s32[]{:T(128)} %clamp.3, (bf16[256,4096]{1,0:T(8,128)(2,1)}, bf16[80,1024]{1,0:T(8,128)(2,1)S(1)}, f32[2,64,256]{2,1,0:T(8,128)S(1)}) %tuple.82, ...), branch_computations={%region_0.1_spmd, %region_1.2_spmd, %region_2.3_spmd, %region_3.4_... | conditional | bytes 8 | solution.py:450
  10.2 157.9 %spread_11.1 = (bf16[2,512,512]{2,1,0:T(8,128)(2,1)S(1)}, bf16[16,80,1024]{2,1,0:T(8,128)(2,1)}, f32[2,256,512]{2,1,0:T(8,128)}) custom-call(bf16[256,4096]{1,0:T(8,128)(2,1)} %get-tuple-element.128.sg, bf16[80,1024]{1,0:T(8,128)(2,1)S(1)} %get-tuple-element.129.qap, f32[2,64,256]{2,1,0:T(8,128)S(1)} %get-tuple-element.130.gt), custom_call_target="tpu_custom_call" | custom-call | tf_op jit(solution)/shard_map/cond/branch_11_fun/spread_11/pallas_call | solution.py:216
  168.4 85.7 %turn.1 = f32[2,64,256]{2,1,0:T(8,128)S(1)} custom-call(bf16[2,512,512]{2,1,0:T(8,128)(2,1)S(1)} %get-tuple-element.143.qg, bf16[16,80,1024]{2,1,0:T(8,128)(2,1)} %get-tuple-element.144.qa, f32[2,256,512]{2,1,0:T(8,128)} %get-tuple-element.145.gx), custom_call_target="tpu_custom_call" | custom-call | tf_op jit(solution)/shard_map/turn/pallas_call | solution.py:410
  254.1 0.7 reverse_select_fusion
  (2 shorter events, 0.0 us)
Async XLA Ops:
  0.0 3.5 %copy-start = (bf16[1,1024,1024]{2,1,0:T(8,128)(2,1)S(1)}, bf16[1,1024,1024]{2,1,0:T(8,128)(2,1)}, u32[]{:S(2)}) copy-start(bf16[1,1024,1024]{2,1,0:T(8,128)(2,1)} %param.22) | copy-start | bytes 6291460

commit v2 on v0

v2 whole, which is shorter than its diff:
```python
import functools

import jax
import jax.numpy as jnp
from jax import lax
from jax.experimental import pallas as pl
from jax.experimental.pallas import tpu as pltpu
from jax.sharding import PartitionSpec as P

DAMPING = 0.1
MESH = pl.DeviceIdType.MESH
NX, NZ, NY, NL, NC = 4, 4, 4, 2, 2
NEAR = NY * NL
FIXED_OWNER = 15
CHUNKS = 8
SLACK = 2
FLIGHT = 2
LAG = 4
READY = CHUNKS + 3 * SLACK + 1
ROWS = 256 // CHUNKS
WIDE = 1024 + 128
BF16, F32, I16 = jnp.bfloat16, jnp.float32, jnp.int16


def coords():
    rep, grp = lax.axis_index("rep"), lax.axis_index("grp")
    return rep // NZ, rep % NZ, grp // (NL * NC), (grp // NC) % NL, grp % NC


def dev(x, zh, y, zl, c):
    return (x * NZ + zh, y * (NL * NC) + zl * NC + c)


def remote(src, dst, ss, rs, to):
    return pltpu.make_async_remote_copy(src_ref=src, dst_ref=dst, send_sem=ss, recv_sem=rs, device_id=to, device_id_type=MESH)


def at(start, size):
    return pl.ds(pl.multiple_of(start, size), size)


def split(value):
    high = value.astype(BF16)
    low = (value - high.astype(F32)).astype(BF16)
    return jnp.concatenate([high, low], axis=0)


def fold(value):
    half = value.shape[0] // 2
    return value[:half] + value[half:]


def code(value):
    top = jnp.maximum(jnp.max(jnp.abs(value), axis=0, keepdims=True), 1e-30)
    scale = top * (1 / 32767)
    digits = jnp.round(value * (32767 / top)).astype(jnp.int32).astype(jnp.int16)
    return digits, jnp.concatenate([scale[:, :128], scale[:, 128:], jnp.zeros((6, 128), F32)], axis=0)


def decode(digits, tile):
    scale = jnp.concatenate([tile[0:1], tile[1:2]], axis=1)
    return digits.astype(jnp.int32).astype(F32) * scale


def dot(left, right, dims=((1,), (0,))):
    return lax.dot_general(left, right, (dims, ((), ())), preferred_element_type=F32)


def kernel(other, owners, store_a, sg, vals_a, vals_g, grads, out, piece, gt, gx, qg, qa, yt, ys, yr, yv, t4, mid, wt, wr, wc, ws, wall, wv, wf, mx, mc, ms,
           orc, rot, qg_ss, qg_rs, fw_ss, qa_ss, qa_rs, qf_ss, ga_ss, ga_rs, gx_ss, gx_rs, gc_ss, gc_rs, loc, y_ss, y_rs, s_ss, s_rs, t_ss, t_rs,
           w_ss, w_rs, a_ss, a_rs, v_ss, v_rs, c_ss, c_rs, o_ss, o_rs):
    x, zh, y, zl, c = coords()
    q = y * NL + zl

    def near(i):
        return (y + i // NL) % NY, (zl + i % NL) % NL

    barrier = pltpu.get_barrier_semaphore()

    def greet(peer):
        pl.semaphore_signal(barrier, inc=1, device_id=peer, device_id_type=MESH)

    @pl.loop(1, NX)
    def _(d):
        greet(dev((x + d) % NX, zh, y, zl, 0))
        greet(dev((x + d) % NX, zh, y, zl, 1))
        greet(dev(x, (zh + d) % NZ, y, zl, c))

    @pl.loop(1, NEAR)
    def _(i):
        ty, tl = near(i)
        greet(dev(x, zh, ty, tl, 0))
        greet(dev(x, zh, ty, tl, 1))

    greet(dev(x, zh, y, zl, 1 - c))

    first = owners[0] == FIXED_OWNER
    gt[0] = jnp.where(first, grads[0], grads[1])
    gt[1] = jnp.where(first, grads[1], grads[0])

    def source(layer):
        return [layer * (other // NZ) + (1 - layer) * (FIXED_OWNER // NZ), layer * (other % NZ) + (1 - layer) * (FIXED_OWNER % NZ)]

    def mine(layer):
        return (x == source(layer)[0]) & (zh == source(layer)[1])

    owner = mine(0) | mine(1)
    owned = jnp.where(mine(1), 1, 0)

    grp = q * NC + c

    @pl.when(owner)
    def _():
        load = pltpu.make_async_copy(store_a.at[0, at(((grp % 4) * 4 + grp // 4) * 64, 64), :], piece.at[:, pl.ds(0, 1024)], loc.at[0])
        load.start()
        va, vg = vals_a[...].astype(F32), vals_g[...].astype(F32)
        lines = [va[:, i * 128:(i + 1) * 128] for i in range(8)] + [vg[:, i * 128:(i + 1) * 128] for i in range(2)]
        piece[:, 1024:WIDE] = jnp.concatenate(lines + [jnp.zeros((54, 128), F32)], axis=0).astype(BF16)
        load.wait()

    pl.semaphore_wait(barrier, 3 * (NX - 1) + 2 * (NEAR - 1) + 1)

    def qa_first(d):
        tx = (x + d) % NX
        return remote(piece.at[at(tx * 16, 16), :], qa.at[y, zl, c, tx], qa_ss.at[d], qa_rs.at[c], dev(tx, zh, y, zl, owned))

    def qg_first(k, d, core):
        tx = (x + d) % NX
        return remote(sg.at[0, at(k * ROWS, ROWS), at((tx * NC + core) * 512, 512)], qg.at[owned, at(c * 256 + k * ROWS, ROWS), :],
                      qg_ss.at[k, d, core], qg_rs.at[owned, c, k], dev(tx, zh, y, zl, core))

    def qg_sent(k):
        for d in (2, 1, 3):
            for core in range(NC):
                qg_first(k, d, core).wait_send()
        qg_first(k, 0, 1 - c).wait_send()

    def qg_local(k):
        return pltpu.make_async_copy(sg.at[0, at(k * ROWS, ROWS), at((x * NC + c) * 512, 512)],
                                     qg.at[owned, at(c * 256 + k * ROWS, ROWS), :], qg_rs.at[owned, c, k])

    tile = at(x * 64, 64), at(c * 256, 256)

    def g_x(l, d):
        return remote(gt.at[l], gx.at[l, tile[0], tile[1]], gx_ss.at[l, d], gx_rs.at[l, d], dev((x + d) % NX, zh, y, zl, c))

    def g_c(l):
        half = gx.at[l, :, tile[1]]
        return remote(half, half, gc_ss.at[l], gc_rs.at[l], dev(x, zh, y, zl, 1 - c))

    @pl.when(owner)
    def _():
        @pl.loop(1, NX)
        def _(d):
            qa_first(d).start()

        @pl.when(c == owned)
        def _():
            pltpu.make_async_copy(piece.at[at(x * 16, 16), :], qa.at[y, zl, c, x], qa_rs.at[c]).start()

        @pl.when(c != owned)
        def _():
            qa_first(0).start()

    def ring(layer, part):
        oz = source(layer)[1]
        return (zh + 1 + 2 * part) % NZ, (1 - part) * ((zh + NZ - oz) % NZ) + part * ((oz + NZ - zh) % NZ)

    def qa_on(part):
        block = qa.at[y, zl, part, x]
        return remote(block, block, qf_ss.at[part], qa_rs.at[part], dev(x, ring(c, part)[0], y, zl, c))

    def qg_on(layer, part, k):
        block = qg.at[layer, at(part * 256 + k * ROWS, ROWS), :]
        return remote(block, block, fw_ss.at[layer, part, k], qg_rs.at[layer, part, k], dev(x, ring(layer, part)[0], y, zl, c))

    def over_x(block, stage):
        return [remote(block, block, ga_ss.at[stage, d], ga_rs.at[stage, d], dev((x + d) % NX, zh, y, zl, c)) for d in (2, 1, 3)]

    def over_y(block, stage):
        return [remote(block, block, ga_ss.at[stage, d], ga_rs.at[stage, d], dev(x, zh, (y + d) % NY, zl, c)) for d in (2, 1, 3)]

    def over_zl(block, stage):
        return [remote(block, block, ga_ss.at[stage, 0], ga_rs.at[stage, 0], dev(x, zh, y, 1 - zl, c))]

    stages = (
        (lambda: over_zl(qa.at[y, zl, :, x], 0), lambda: over_y(qa.at[y, :, :, x], 1), lambda: over_x(qa.at[:, :, :, x], 2)),
        (lambda: over_x(qa.at[y, zl, :, x], 0), lambda: over_zl(qa.at[y, zl], 1), lambda: over_y(qa.at[y], 2)),
    )

    def per_core(act):
        for core in range(NC):
            @pl.when(c == core)
            def _():
                act(stages[core])

    def gather_start(stage):
        def act(mine):
            if stage:
                for copy in mine[stage - 1]():
                    copy.wait_recv()
            for copy in mine[stage]():
                copy.start()
        per_core(act)

    def y_copy(l, i):
        ty, tl = near(i)
        tq = ty * NL + tl
        return [remote(yt.at[l, tq], yr.at[q, c], y_ss.at[l, i], y_rs.at[i, c], dev(x, zh, ty, tl, l)),
                remote(ys.at[l, tq], yv.at[q, c], s_ss.at[l, i], s_rs.at[i, c], dev(x, zh, ty, tl, l))]

    @pl.loop(0, READY + LAG + 1)
    def _(t):
        @pl.when(owner & (t < CHUNKS))
        def _():
            @pl.when(t >= FLIGHT)
            def _():
                qg_sent(t - FLIGHT)
            for d in (2, 1, 3):
                for core in range(NC):
                    qg_first(t, d, core).start()
            qg_first(t, 0, 1 - c).start()
            qg_local(t).start()

        @pl.loop(0, 2)
        def _(part):
            away = ring(c, part)[1]

            @pl.when(away * SLACK == t)
            def _():
                qa_on(part).wait_recv()

                @pl.when(away < NZ - 1)
                def _():
                    qa_on(part).start()

        @pl.loop(0, 4)
        def _(flow):
            layer, part = flow // 2, flow % 2
            away = ring(layer, part)[1]
            k = t - 1 - SLACK * away - LAG * layer

            @pl.when((k >= 0) & (k < CHUNKS))
            def _():
                qg_on(layer, part, k).wait_recv()

                @pl.when(away < NZ - 1)
                def _():
                    @pl.when(k >= FLIGHT)
                    def _():
                        qg_on(layer, part, k - FLIGHT).wait_send()
                    qg_on(layer, part, k).start()

        @pl.when(t == 3)
        def _():
            @pl.loop(0, 2)
            def _(l):
                @pl.loop(1, NX)
                def _(d):
                    g_x(l, d).start()
                gx[l, tile[0], tile[1]] = gt[l]

        for stage, when in enumerate((7, 8, 9)):
            @pl.when(t == when)
            def _():
                gather_start(stage)

        @pl.when(t == READY - 3)
        def _():
            @pl.loop(0, 2)
            def _(l):
                @pl.loop(1, NX)
                def _(d):
                    g_x(l, d).wait_recv()
                g_c(l).start()

        @pl.when((t == READY) | (t == READY + LAG))
        def _():
            l = (t - READY) // LAG
            g_c(l).wait_recv()
            both = split(gx[l])

            @pl.loop(0, 4)
            def _(h):
                part = fold(dot(both, qg[l, :, at(h * 128, 128)])).T
                for k in range(2):
                    yt[l, h * 2 + k], ys[l, h * 2 + k] = code(part[k * 64:(k + 1) * 64])

            @pl.loop(1, NEAR)
            def _(i):
                for copy in y_copy(l, i):
                    copy.start()

            @pl.when(c == l)
            def _():
                yr[q, l] = yt[l, q]
                yv[q, l] = ys[l, q]

            @pl.when(c != l)
            def _():
                for copy in y_copy(l, 0):
                    copy.start()

    def y_wait(i, k):
        sq = ((y + NY - i // NL) % NY) * NL + (zl + i % NL) % NL
        remote(yr.at[sq, k], yr.at[sq, k], y_ss.at[0, i], y_rs.at[i, k], dev(x, zh, y, zl, 1 - c)).wait_recv()
        remote(yv.at[sq, k], yv.at[sq, k], s_ss.at[0, i], s_rs.at[i, k], dev(x, zh, y, zl, 1 - c)).wait_recv()

    y_wait(0, 1 - c)

    @pl.loop(1, NEAR)
    def _(i):
        for k in range(NC):
            y_wait(i, k)

    @pl.loop(0, NC)
    def _(k):
        t4[at(k * 64, 64), :] = lax.fori_loop(0, NEAR, lambda i, total: total + decode(yr[i, k], yv[i, k]), jnp.zeros((64, 256), F32))

    def t_copy(d):
        to = (zh + d) % NZ
        return remote(t4.at[at(to * 32, 32), :], mid.at[zh], t_ss.at[d], t_rs.at[d], dev(x, to, y, zl, c))

    for d in range(1, NZ):
        t_copy(d).start()
    mid[zh] = t4[at(zh * 32, 32), :]
    for d in range(1, NZ):
        t_copy(d).wait_recv()

    def act(mine):
        for copy in mine[2]():
            copy.wait_recv()
    per_core(act)

    spec_a = jnp.concatenate([qa[0, 0, 0, 0, :, 1024:WIDE].astype(F32)[i:i + 1] for i in range(8)], axis=1)
    spot = (x * 2 + zh // 2) * 2 + q // 4
    line = qa[spot // 4, (spot // 2) % 2, spot % 2, 0, :, 1024:WIDE].astype(F32)
    line = jnp.concatenate([line[8:9], line[9:10]], axis=1)
    start = (q % 4) * 64 + (zh % 2) * 32
    pick = lax.broadcasted_iota(jnp.int32, (32, 256), 1) == lax.broadcasted_iota(jnp.int32, (32, 256), 0) + start
    spec_g = jnp.sum(jnp.where(pick, line, 0.0), axis=1, keepdims=True)
    turned = split(jnp.concatenate([mid[k] for k in range(NZ)], axis=1))

    @pl.loop(0, 4)
    def _(k):
        rot[k] = fold(dot(turned, qa[:, :, :, :, :, at(k * 256, 256)].reshape(1024, 256)))

    rotated = jnp.concatenate([rot[k] for k in range(4)], axis=1)
    scaled = split(rotated / (spec_g * spec_a + DAMPING))

    @pl.loop(0, 4)
    def _(k):
        wt[k] = fold(dot(scaled, qa[k, :, :, :, :, 0:1024].reshape(256, 1024), ((1,), (1,))))

    def w_copy(d):
        to = (zh + d) % NZ
        return remote(wt.at[to], wr.at[at(zh * 32, 32), :], w_ss.at[d], w_rs.at[d], dev(x, to, y, zl, c))

    for d in range(1, NZ):
        w_copy(d).start()
    wr[at(zh * 32, 32), :] = wt[zh]
    for d in range(1, NZ):
        w_copy(d).wait_recv()

    def a_copy(k, i):
        ty, tl = near(i)
        return [remote(wc.at[k], wall.at[c, q], a_ss.at[k, i], a_rs.at[c, i], dev(x, zh, ty, tl, k)),
                remote(ws.at[k], wv.at[c, q], v_ss.at[k, i], v_rs.at[c, i], dev(x, zh, ty, tl, k))]

    for k in range(NC):
        wc[k], ws[k] = code(wr[k * 64:(k + 1) * 64, :])

    @pl.loop(1, NEAR)
    def _(i):
        for k in range(NC):
            for copy in a_copy(k, i):
                copy.start()
    for copy in a_copy(1 - c, 0):
        copy.start()
    wall[c, q] = wc[c]
    wv[c, q] = ws[c]

    def c_copy(l):
        return remote(mx.at[l, 1 - c], mc.at[l], c_ss.at[l], c_rs.at[l], dev(x, zh, y, zl, 1 - c))

    def o_copy(l, d):
        to = (x + d) % NX
        return remote(ms.at[l, at(to * 64, 64), :], orc.at[l, x], o_ss.at[l, d], o_rs.at[l, d], dev(to, zh, y, zl, c))

    def a_wait(l, i):
        sq = ((y + NY - i // NL) % NY) * NL + (zl + i % NL) % NL
        remote(wall.at[l, sq], wall.at[l, sq], a_ss.at[0, i], a_rs.at[l, i], dev(x, zh, y, zl, 1 - c)).wait_recv()
        remote(wv.at[l, sq], wv.at[l, sq], v_ss.at[0, i], v_rs.at[l, i], dev(x, zh, y, zl, 1 - c)).wait_recv()

    @pl.loop(0, 2)
    def _(l):
        @pl.when(c != l)
        def _():
            a_wait(l, 0)

        @pl.loop(1, NEAR)
        def _(i):
            a_wait(l, i)

        @pl.loop(0, NEAR)
        def _(i):
            wf[at(i * 64, 64), :] = decode(wall[l, i], wv[l, i])
        both = split(wf[...].T)

        @pl.loop(0, 2)
        def _(h):
            mx[l, h] = fold(dot(both, qg[l, at(h * 256, 256), :], ((1,), (1,))))
        c_copy(l).start()

    for l in range(2):
        c_copy(l).wait_recv()
        ms[l] = mx[l, c] + mc[l]

        @pl.loop(1, NX)
        def _(d):
            o_copy(l, d).start()
        orc[l, x] = ms[l, at(x * 64, 64), :]
    for l in range(2):
        @pl.loop(1, NX)
        def _(d):
            o_copy(l, d).wait_recv()
        out[l] = (orc[l, 0] + orc[l, 1]) + (orc[l, 2] + orc[l, 3])

    @pl.loop(0, 2)
    def _(l):
        @pl.loop(1, NEAR)
        def _(i):
            for copy in y_copy(l, i) + a_copy(l, i):
                copy.wait_send()
        c_copy(l).wait_send()
        g_c(l).wait_send()

        @pl.loop(1, NX)
        def _(d):
            o_copy(l, d).wait_send()
            g_x(l, d).wait_send()
    for copy in y_copy(1 - c, 0) + a_copy(1 - c, 0):
        copy.wait_send()
    for d in range(1, NZ):
        t_copy(d).wait_send()
        w_copy(d).wait_send()

    def act(mine):
        for stage in range(3):
            for copy in mine[stage]():
                copy.wait_send()
    per_core(act)

    @pl.loop(0, 2)
    def _(part):
        @pl.when(ring(c, part)[1] < NZ - 1)
        def _():
            qa_on(part).wait_send()

    @pl.loop(0, 4)
    def _(flow):
        layer, part = flow // 2, flow % 2

        @pl.when(ring(layer, part)[1] < NZ - 1)
        def _():
            @pl.loop(CHUNKS - FLIGHT, CHUNKS)
            def _(k):
                qg_on(layer, part, k).wait_send()

    @pl.when(owner)
    def _():
        @pl.loop(1, NX)
        def _(d):
            qa_first(d).wait_send()

        @pl.when(c != owned)
        def _():
            qa_first(0).wait_send()

        for k in range(CHUNKS - FLIGHT, CHUNKS):
            qg_sent(k)


def run(other, owners, store_a, store_g, vals_a, vals_g, grads):
    dma = pltpu.SemaphoreType.DMA
    vmem, anywhere = pl.BlockSpec(memory_space=pltpu.VMEM), pl.BlockSpec(memory_space=pl.ANY)
    return pl.pallas_call(
        functools.partial(kernel, other),
        out_shape=jax.ShapeDtypeStruct((2, 64, 256), F32),
        in_specs=[pl.BlockSpec(memory_space=pltpu.SMEM), anywhere, anywhere, vmem, vmem, vmem],
        out_specs=vmem,
        scratch_shapes=[
            pltpu.VMEM((64, WIDE), BF16),
            pltpu.VMEM((2, 64, 256), F32),
            pltpu.VMEM((2, 256, 512), F32),
            pltpu.VMEM((2, 512, 512), BF16),
            pltpu.VMEM((NY, NL, NC, NX, 16, WIDE), BF16),
            pltpu.VMEM((2, NEAR, 64, 256), I16),
            pltpu.VMEM((2, NEAR, 8, 128), F32),
            pltpu.VMEM((NEAR, 2, 64, 256), I16),
            pltpu.VMEM((NEAR, 2, 8, 128), F32),
            pltpu.VMEM((128, 256), F32),
            pltpu.VMEM((4, 32, 256), F32),
            pltpu.VMEM((4, 32, 256), F32),
            pltpu.VMEM((128, 256), F32),
            pltpu.VMEM((2, 64, 256), I16),
            pltpu.VMEM((2, 8, 128), F32),
            pltpu.VMEM((2, NEAR, 64, 256), I16),
            pltpu.VMEM((2, NEAR, 8, 128), F32),
            pltpu.VMEM((512, 256), F32),
            pltpu.VMEM((2, 2, 256, 256), F32),
            pltpu.VMEM((2, 256, 256), F32),
            pltpu.VMEM((2, 256, 256), F32),
            pltpu.VMEM((2, 4, 64, 256), F32),
            pltpu.VMEM((4, 32, 256), F32),
            dma((CHUNKS, NX, NC)), dma((2, NC, CHUNKS)), dma((2, 2, CHUNKS)),
            dma((NX,)), dma((2,)), dma((2,)), dma((3, 4)), dma((3, 4)),
            dma((2, 4)), dma((2, 4)), dma((2,)), dma((2,)), dma((1,)),
            dma((2, 8)), dma((8, 2)), dma((2, 8)), dma((8, 2)), dma((4,)), dma((4,)), dma((4,)), dma((4,)),
            dma((2, 8)), dma((2, 8)), dma((2, 8)), dma((2, 8)),
            dma((2,)), dma((2,)), dma((2, 4)), dma((2, 4)),
        ],
        compiler_params=pltpu.CompilerParams(collective_id=other, has_side_effects=True, vmem_limit_bytes=40 * 2**20),
        name=f"kfac_{other}",
    )(owners, store_a, store_g, vals_a, vals_g, grads)


def local(owners, store_a, store_g, vals_a, vals_g, grads):
    first = owners[0] == FIXED_OWNER
    other = jnp.where(first, owners[1], owners[0])
    variants = [functools.partial(run, k) for k in range(FIXED_OWNER)]
    result = lax.switch(other, variants, owners, store_a, store_g, vals_a, vals_g, grads)
    return jnp.where(first, result, result[::-1])


def solution(mesh):
    return jax.shard_map(
        local,
        mesh=mesh,
        in_specs=(
            P(),
            P("rep", None, None),
            P("rep", "grp", None),
            P("rep", None),
            P("rep", "grp"),
            P(None, "rep", "grp"),
        ),
        out_specs=P(None, "rep", "grp"),
        check_vma=False,
    )
```

time: 897 us -> 119 us (0.13)
  waiting for transfers between devices: 803 us -> 0 us
  Pallas kernels: 0 us -> 110 us
  blocking collectives: 38.2 us -> 0 us
  matrix products: 26.4 us -> 0 us
  between operations: 14.6 us -> 1.93 us
  other arithmetic: 10.2 us -> 0.67 us
    reduce_scatter x6 -> x0, waiting for transfers between devices: 424 us -> none  [the longest x2 169 us: local(): lax.psum_scatter(jnp.dot(block, mixed, precision=highest, preferred_eleme...]
    psum x1 -> x0, waiting for transfers between devices: 232 us -> none  [broadcast(): return lax.psum(kept, axis)]
    all_gather x4 -> x0, waiting for transfers between devices: 146 us -> none  [the longest x2 80.1 us: local(): lax.all_gather(got_rows, 'grp', axis=0, tiled=True).astype(jnp.float32)]
    pallas_call x0 -> x1, Pallas kernels: none -> 110 us  [run(): pl.pallas_call(functools.partial(kernel, other), out_shape=jax.ShapeDtype...]
    psum x1 -> x0, blocking collectives: 38.2 us -> none  [broadcast(): return lax.psum(kept, axis)]
    dot_general x8 -> x0, matrix products: 26.4 us -> none  [the longest x2 8.9 us: local(): lax.dot_general(basis_g, tile, (((0,), (1,)), ((), ())), precision=highes...]
  transfers between devices with their start and end apart: 11 -> 0, of which waited for: 11 -> 0; matrix products, arithmetic and copies ran while one was open for 3% -> 0% of each run, Pallas kernels for 0% -> 0%
where the time goes in v2:
time: 119 us
  Pallas kernels  110 us (92%)
  loops' own time  5.13 us (4%)
  between operations  1.93 us (2%)
  local copies, waits for them, and re-layouts  1.31 us (1%)
    pallas_call x1, Pallas kernels, run(): pl.pallas_call(functools.partial(kernel, other), out_shape=jax.ShapeDtype...  110 us
    another operation x1, loops' own time, local(): lax.switch(other, variants, owners, store_a, store_g, vals_a, vals_g, grads)  5.13 us

profile of v2, /device:TPU:1, one launch (start us, length us, event | category | flops | bytes accessed | tf_op | source)
XLA Modules:
  0.0 118.6 jit_solution(5391614062775360911)
XLA Ops:
  0.0 1.3 %fusion = (s32[1]{0:T(128)}, s32[1]{0:T(128)}) fusion(s32[2]{0:T(128)} %param.21), kind=kLoop, calls=%fused_computation.1 | loop fusion | bytes 16 | tf_op jit(solution)/shard_map/slice | solution.py:530
  3.2 114.7 %conditional.1 = (f32[2,64,256]{2,1,0:T(8,128)S(1)}) conditional(s32[]{:T(128)} %clamp.3, (s32[2]{0:T(128)}, bf16[1,1024,1024]{2,1,0:T(8,128)(2,1)}, bf16[1,256,4096]{2,1,0:T(8,128)(2,1)}, bf16[1,1024]{1,0:T(2,128)(2,1)}, bf16[1,256]{1,0:T(2,128)(2,1)}, /*index=5*/f32[2,64,256]{2,1,0:T(8,128)}) %tuple.50, ...), branch_computations={%region_0.1_spmd, %region_1.2_spmd, %region_2.3_spmd, %region_3.4_... | conditional | bytes 8 | solution.py:532
  7.8 109.6 %kfac_6.1 = f32[2,64,256]{2,1,0:T(8,128)S(1)} custom-call(s32[2]{0:T(128)} %get-tuple-element.237.owners, bf16[1,1024,1024]{2,1,0:T(8,128)(2,1)} %get-tuple-element.238.store_a, bf16[1,256,4096]{2,1,0:T(8,128)(2,1)} %get-tuple-element.239.sg, bf16[1,1024]{1,0:T(2,128)(2,1)} %get-tuple-element.240.vals_a, bf16[1,256]{1,0:T(2,128)(2,1)} %get-tuple-element.241.vals_g, ...), custom_call_target="tpu_custom_call" | custom-call | tf_op jit(solution)/shard_map/cond/branch_6_fun/kfac_6/pallas_call | solution.py:487
  117.9 0.7 reverse_select_fusion
